TPU v7x, 128 devices: a whole 4x4x4 slice. The times are simulated.
128 devices in a mesh: cuts: 16 (over y, x_hi, core), col: 8 (over z, x_lo).
Axes of the slice: x: 4 (x_hi: 2, x_lo: 2; x = x_hi * 2 + x_lo), y: 4, z: 4, core: 2. Of those that a mesh axis runs over, the one named last changes fastest.
Arguments:
- records: float32 [192, 512, 8192], P('cuts', None, 'col'), may hold values from -6 to 6
- row_lengths: int32 [192], P('cuts'), may hold values from 128 to 512, as said below
- row_mask: int32 [192, 512], P('cuts'), may hold values 0 or 1
- core_init: float32 [64, 64], replicated, may hold values from -6 to 6
- column_init: float32 [64, 8192], P(None, 'col'), may hold values from -6 to 6
- weight_init: float32 [192, 64], P('cuts'), may hold values from -6 to 6
Outputs:
- core_out: float32 [64, 64], replicated
- column_out: float32 [64, 8192], P(None, 'col')
- weight_out: float32 [192, 64], P('cuts')
Inputs may be any that keep to these rules, and one draw needn't show every extreme that they name: Each slice uses its first row_lengths rows; some slice uses all 512.
All inputs are finite; a program needn't handle non-finite values. No bound on the sum of `row_mask` on one device may be relied on, other than what follows from the above.
Results may differ from a plain program's by a relative error of at most 0.0003.
Values sent between devices are 32-bit elements; how exact they have to be, the bound alone decides.
A program may use at most 128 MiB of HBM per device.

v0:
```python
import jax
import jax.numpy as jnp
from jax import lax
from jax.sharding import PartitionSpec as P

R = 64
J = 8192
NS_STEPS = 8


HP = lax.Precision.HIGHEST


def solve_sym(gram, rhs):
    lower = jnp.linalg.cholesky(gram)
    inner = lax.linalg.triangular_solve(lower, rhs, left_side=True, lower=True)
    return lax.linalg.triangular_solve(lower, inner, left_side=True, lower=True, transpose_a=True)


def newton_steps(start, gram_sum):
    current = start
    for step in range(NS_STEPS):
        gram = gram_sum(jnp.einsum("kai,kbi->kab", current, current, precision=HP))
        current = 1.5 * current - 0.5 * jnp.einsum("kab,kbi->kai", gram, current, precision=HP)
    return current


def shards(records, row_lengths, row_mask, core_init, column_init, weight_init):
    slots = records.shape[1]
    rows = lax.broadcasted_iota(jnp.int32, (records.shape[0], slots), 1)
    valid = ((rows < row_lengths[:, None]) & (row_mask == 1)).astype(jnp.float32)
    masked = records * valid[:, :, None]
    partial_value = jnp.einsum("rj,kij->kri", column_init, masked, precision=HP)
    summed = lax.psum(partial_value, "col")
    mixed = jnp.einsum("ar,kri->kai", core_init, weight_init[:, :, None] * summed, precision=HP)
    scale = jnp.sqrt(jnp.sum(mixed * mixed, axis=(1, 2)) + 1e-06)
    polar = newton_steps(mixed / scale[:, None, None], lambda gram: gram)
    projected = jnp.einsum("kai,kij->kaj", polar, masked, precision=HP)
    slice_gram = lax.psum(jnp.dot(weight_init.T, weight_init, precision=HP), "cuts")
    column_gram = lax.psum(jnp.dot(column_init, column_init.T, precision=HP), "col")
    zterm = jnp.einsum("kaj,rj->kar", projected, column_init, precision=HP)
    h_local = jnp.einsum("kar,kr->ar", zterm, weight_init, precision=HP)
    h_terms = lax.psum(h_local, ("cuts", "col"))
    core = solve_sym(slice_gram * column_gram, h_terms.T).T
    core_n = core / jnp.sqrt(jnp.sum(core * core, axis=0) + 1e-06)[None, :]
    tproj = jnp.einsum("ar,kaj->krj", core_n, projected, precision=HP)
    v_local = jnp.einsum("kr,krj->rj", weight_init, tproj, precision=HP)
    core_gram = jnp.dot(core_n.T, core_n, precision=HP)
    system = slice_gram * core_gram
    v_terms = lax.psum(v_local, "cuts")
    vt = solve_sym(system, v_terms)
    v_gram = lax.psum(jnp.dot(vt, vt.T, precision=HP), "col")
    norms = jnp.sqrt(jnp.diagonal(v_gram) + 1e-06)
    column_n = vt / norms[:, None]
    vn_gram = v_gram / (norms[:, None] * norms[None, :])
    w_local = jnp.einsum("krj,rj->kr", tproj, column_n, precision=HP)
    w_terms = lax.psum(w_local, "col")
    weight_out = solve_sym(core_gram * vn_gram, w_terms.T).T
    return (core_n * jnp.sqrt(jnp.float32(R)), column_n * jnp.sqrt(jnp.float32(J)), weight_out)


def solution(mesh):
    in_specs = (
        P("cuts", None, "col"),
        P("cuts"),
        P("cuts", None),
        P(),
        P(None, "col"),
        P("cuts", None),
    )
    out_specs = (P(), P(None, "col"), P("cuts", None))
    return jax.shard_map(shards, mesh=mesh, in_specs=in_specs, out_specs=out_specs, check_vma=False)
```

profile of v0, /device:TPU:0, one launch (start us, length us, event | category | flops | bytes accessed | tf_op | source)
XLA Modules:
  0.0 532.4 jit_solution(1031676666560155095)
XLA Ops:
  7.2 0.9 fusion.49
  8.1 30.7 %fusion.15 = f32[12,64,512]{2,1,0:T(8,128)} fusion(f32[12,512,1024]{2,1,0:T(8,128)} %param.7, f32[12,512]{1,0:T(8,128)S(1)} %fusion.49, f32[64,1024]{1,0:T(8,128)S(1)} %copy-done), kind=kOutput, calls=%fused_computation.25 | convolution fusion | flops 4838129664 | bytes 27025408 | tf_op jit(solution)/shard_map/rj,kij->kri/dot_general | solution.py:33
  39.8 70.9 %psum.49 = f32[64,64]{0,1:T(8,128)S(1)} all-reduce(f32[64,64]{0,1:T(8,128)S(1)} %fusion.54), channel_id=1, replica_groups=mesh['cuts'=16,'col'=8] {'cuts'}, use_global_device_ids=true, to_apply=%region_0.0 | all-reduce | flops 4096 | bytes 32768 | tf_op jit(solution)/shard_map/psum | solution.py:39
  111.0 34.8 %psum.50 = f32[64,64]{0,1:T(8,128)S(1)} all-reduce(f32[64,64]{0,1:T(8,128)S(1)} %fusion.55), channel_id=1, replica_groups=mesh['cuts'=16,'col'=8] {'col'}, use_global_device_ids=true, to_apply=%region_1.0 | all-reduce | flops 4096 | bytes 32768 | tf_op jit(solution)/shard_map/psum | solution.py:40
  145.9 5.8 %cholesky.59 = f32[64,64]{1,0:T(8,128)S(1)} custom-call(f32[64,64]{1,0:T(8,128)S(1)} %fusion.47), custom_call_target="Cholesky" | custom-call | tf_op jit(solution)/shard_map/jit(cholesky)/cholesky | solution.py:15
  152.4 0.7 fusion.28
  153.1 5.5 %custom-call.17 = f32[1,64,64]{1,2,0:T(8,128)} custom-call(f32[1,64,64]{2,1,0:T(8,128)S(1)} %fusion.28), custom_call_target="InvertDiagBlocksLowerTriangular" | custom-call | tf_op jit(solution)/shard_map/triangular_solve | solution.py:17
  158.7 3.2 multiply_reduce_fusion
  161.9 1.8 fusion.23
  163.7 1.7 bitcast_subtract_fusion
  165.4 1.6 fusion.56
  167.0 1.6 multiply_subtract_fusion.5
  168.6 1.6 fusion.57
  170.2 2.0 multiply_subtract_fusion.4
  172.2 1.6 fusion.58
  173.8 1.6 multiply_subtract_fusion.3
  175.4 1.6 fusion.59
  176.9 1.6 multiply_subtract_fusion.2
  178.5 1.6 fusion.60
  180.1 1.6 multiply_subtract_fusion.1
  181.7 1.6 fusion.61
  183.3 1.8 multiply_subtract_fusion
  185.0 1.6 fusion.62
  186.6 2.5 fusion.63
  189.2 21.3 %fusion = f32[12,64,1024]{2,1,0:T(8,128)S(1)} fusion(f32[12,512,1024]{2,1,0:T(8,128)} %param.7, f32[12,512]{1,0:T(8,128)S(1)} %fusion.49, f32[12,64,512]{2,1,0:T(8,128)} %fusion.63, f32[12,64,512]{2,1,0:T(8,128)S(1)} %multiply_subtract_fusion), kind=kOutput, calls=%fused_computation.1 | convolution fusion | flops 4839309312 | bytes 31481856 | tf_op jit(solution)/shard_map/kai,kij->kaj/dot_general | solution.py:38
  210.5 1.7 copy-done.1
  212.1 2.6 fusion.19
  214.8 62.8 %psum.52 = f32[64,64]{0,1:T(8,128)S(1)} all-reduce(f32[64,64]{0,1:T(8,128)S(1)} %bitcast.120), channel_id=1, replica_groups=mesh['cuts'=16,'col'=8] {'cuts','col'}, use_global_device_ids=true, to_apply=%region_6.0 | all-reduce | flops 4096 | bytes 32768 | tf_op jit(solution)/shard_map/psum | solution.py:43
  277.9 1.0 multiply_reduce_fusion.1
  278.9 0.9 fusion.53
  279.8 5.7 %convolution_bitcast_fusion = f32[12,64,1024]{2,1,0:T(8,128)S(1)} fusion(f32[12,64,1024]{2,1,0:T(8,128)} %copy-done.1, f32[64,64]{1,0:T(8,128)S(1)} %get-tuple-element.9, f32[64]{0:T(128)S(1)} %add_sqrt_fusion.1), kind=kOutput, calls=%fused_computation.11 | convolution fusion | flops 603983872 | bytes 6308096 | tf_op jit(solution)/shard_map/ar,kaj->krj/dot_general | solution.py:46
  286.2 6.6 %cholesky.70 = f32[64,64]{1,0:T(8,128)S(1)} custom-call(f32[64,64]{1,0:T(8,128)} %fusion.41), custom_call_target="Cholesky" | custom-call | tf_op jit(solution)/shard_map/jit(cholesky)/cholesky | solution.py:15
  293.5 5.5 %fusion.8 = f32[64,1,1024]{2,1,0:T(1,128)S(1)} fusion(f32[12,64,1]{0,2,1:T(1,128)S(1)} %copy.39, f32[12,64,1024]{2,1,0:T(8,128)S(1)} %convolution_bitcast_fusion), kind=kOutput, calls=%fused_computation.9 | convolution fusion | flops 9437184 | bytes 3410944 | tf_op jit(solution)/shard_map/kr,krj->rj/dot_general | solution.py:47
  299.0 0.8 copy.53
  299.8 0.7 fusion.29
  300.4 4.9 custom-call.18
  306.0 127.5 %all-reduce.5.cloned.1.call-done = f32[64,1024]{1,0:T(8,128)} async-done(((f32[64,1024]{1,0:T(8,128)}), f32[64,1024]{1,0:T(8,128)}) %all-reduce.5.cloned.1.call-update) | async-done | bytes 262160 | tf_op jit(solution)/shard_map/psum | solution.py:50
  433.4 1.4 fusion.39
  435.2 0.7 copy-done.2
  436.2 34.6 %psum.54 = f32[64,64]{0,1:T(8,128)S(1)} all-reduce(f32[64,64]{0,1:T(8,128)S(1)} %fusion.64), channel_id=1, replica_groups=mesh['cuts'=16,'col'=8] {'col'}, use_global_device_ids=true, to_apply=%region_9.11 | all-reduce | flops 4096 | bytes 32768 | tf_op jit(solution)/shard_map/psum | solution.py:52
  470.8 0.8 gather_fusion
  471.6 1.9 fusion.27
  473.6 5.8 %cholesky.81 = f32[64,64]{1,0:T(8,128)S(1)} custom-call(f32[64,64]{1,0:T(8,128)S(1)} %fusion.35), custom_call_target="Cholesky" | custom-call | tf_op jit(solution)/shard_map/jit(cholesky)/cholesky | solution.py:15
  480.2 0.7 fusion.30
  480.8 4.9 custom-call.19
  485.7 7.5 %fusion.6 = f32[64,1,12]{2,1,0:T(1,128)S(1)} fusion(f32[12,64,1024]{2,1,0:T(8,128)S(1)} %convolution_bitcast_fusion, f32[64,1024,1]{1,0,2:T(8,128)} %get-tuple-element.4), kind=kOutput, calls=%fused_computation.7 | convolution fusion | flops 9437184 | bytes 3410944 | tf_op jit(solution)/shard_map/krj,rj->kr/dot_general | solution.py:56
  493.2 30.8 %psum.55 = f32[12,64]{0,1:T(8,128)S(1)} all-reduce(f32[12,64]{0,1:T(8,128)S(1)} %bitcast.119), channel_id=1, replica_groups=mesh['cuts'=16,'col'=8] {'col'}, use_global_device_ids=true, to_apply=%region_10.12 | all-reduce | flops 768 | bytes 6144 | tf_op jit(solution)/shard_map/psum | solution.py:57
  524.3 0.8 fusion.31
  (44 shorter events, 6.4 us)
Async XLA Ops:
  7.2 1.0 copy-start
  7.2 151.5 %all-reduce.3.cloned.1.call-start = ((), (), s32[]{:S(2)}) async-start(), calls=%async_computation | async-start | bytes 3145728 | tf_op jit(solution)/shard_map/psum | solution.py:34
  38.8 0.7 copy-start.5
  38.8 119.9 %copy-start.6 = (f32[64,64]{1,0:T(8,128)S(1)}, f32[64,64]{1,0:T(8,128)}, u32[]{:S(2)}) copy-start(f32[64,64]{1,0:T(8,128)} %param.10) | copy-start | bytes 49156
  38.9 394.6 %all-reduce.5.cloned.1.call-start = ((), (), s32[]{:S(2)}) async-start(), calls=%async_computation.1 | async-start | bytes 524288 | tf_op jit(solution)/shard_map/psum | solution.py:50
  210.4 1.7 copy-start.1
  212.1 65.5 %copy-start.3 = (f32[1,64,64]{1,2,0:T(8,128)S(1)}, f32[1,64,64]{1,2,0:T(8,128)}, u32[]{:S(2)}) copy-start(f32[1,64,64]{1,2,0:T(8,128)} %custom-call.17) | copy-start | bytes 49156
  305.3 168.1 %copy-start.4 = (f32[64,64]{0,1:T(8,128)S(1)}, f32[64,64]{0,1:T(8,128)}, u32[]{:S(2)}) copy-start(f32[64,64]{0,1:T(8,128)} %get-tuple-element.11) | copy-start | bytes 49156
  435.1 0.7 copy-start.2
Sparse Core Ops, SparseCore 0:
  39.0 91.0 all-reduce.2
  299.9 133.4 all-reduce.4
where the time goes:
time: 540 us; the launch traced here: 532 us
  blocking collectives  234 us (43%)
  waiting for transfers between devices  128 us (24%)
  matrix products  109 us (20%)
  other arithmetic  41.7 us (8%)
  between operations  14.8 us (3%)
    psum x1, waiting for transfers between devices, shards(): v_terms = lax.psum(v_local, 'cuts')  127 us
    psum x1, blocking collectives, shards(): lax.psum(jnp.dot(weight_init.T, weight_init, precision=HP), 'cuts')  70.9 us
    psum x1, blocking collectives, shards(): h_terms = lax.psum(h_local, ('cuts', 'col'))  62.8 us
    psum x1, blocking collectives, shards(): lax.psum(jnp.dot(column_init, column_init.T, precision=HP), 'col')  34.8 us
    psum x1, blocking collectives, shards(): v_gram = lax.psum(jnp.dot(vt, vt.T, precision=HP), 'col')  34.6 us
    psum x1, blocking collectives, shards(): w_terms = lax.psum(w_local, 'col')  30.8 us
    dot_general x1, matrix products, shards(): partial_value = jnp.einsum('rj,kij->kri', column_init, masked, precision=HP)  30.7 us
    dot_general x1, matrix products, shards(): projected = jnp.einsum('kai,kij->kaj', polar, masked, precision=HP)  21.3 us
  transfers between devices with their start and end apart: 2, of which 1 were waited for; matrix products, arithmetic and copies ran while one was open for 4% of the time, Pallas kernels for 0%

commit v1 on v0

v1 whole, which is shorter than its diff:
```python
import functools

import jax
import jax.numpy as jnp
from jax import lax
from jax.experimental import pallas as pl
from jax.experimental.pallas import tpu as pltpu
from jax.sharding import PartitionSpec as P

R = 64
NS_STEPS = 8
CUTS = 16
COL = 8
SLICES = 12
SLOTS = 512
WIDTH = 1024
HALF = 256

F32 = jnp.float32
BF16 = jnp.bfloat16
HP = lax.Precision.HIGHEST
MESH = pl.DeviceIdType.MESH


def dot(a, b, ca=1, cb=0, precision=HP):
    return lax.dot_general(
        a, b, (((ca,), (cb,)), ((), ())), precision=precision, preferred_element_type=F32
    )


def fast(a, b, ca=1, cb=0):
    return dot(a, b, ca, cb, lax.Precision.DEFAULT)


def halves(x):
    high = x.astype(BF16)
    return high, (x - high.astype(F32)).astype(BF16)


def three(a, b_high, b_low, cb=0):
    a_high, a_low = halves(a)
    rows = a.shape[0]
    both = fast(jnp.concatenate([a_high, a_low], axis=0), b_high, 1, cb)
    return both[:rows] + both[rows:] + fast(a_high, b_low, 1, cb)


def iotas(shape):
    return lax.broadcasted_iota(jnp.int32, shape, 0), lax.broadcasted_iota(jnp.int32, shape, 1)


def diagonals(a):
    rows, cols = iotas(a.shape)
    kept = jnp.where(rows == cols, a, 0.0)
    return jnp.sum(kept, axis=0, keepdims=True), jnp.sum(kept, axis=1, keepdims=True)


def inverse(gram):
    rows, cols = iotas(gram.shape)
    d_row, d_col = diagonals(gram)
    s_row, s_col = lax.rsqrt(d_row), lax.rsqrt(d_col)

    def sweep(p, a):
        at_row, at_col = rows == p, cols == p
        row = jnp.sum(jnp.where(at_row, a, 0.0), axis=0, keepdims=True)
        col = jnp.sum(jnp.where(at_col, a, 0.0), axis=1, keepdims=True)
        pivot = jnp.sum(jnp.where(rows[:, :1] == p, col, 0.0), axis=0, keepdims=True)
        inv = 1.0 / pivot
        scaled = row * inv
        inner = a - col * scaled
        out = jnp.where(at_row, scaled, jnp.where(at_col, -col * inv, inner))
        return jnp.where(at_row & at_col, inv, out)

    return lax.fori_loop(0, R, sweep, gram * s_col * s_row) * s_col * s_row


def kernel(
    rec_ref, len_ref, mask_ref, core_ref, column_ref, weight_ref,
    core_out, column_out, weight_out,
    slab, vmask, psend, precv, pall, sgram, nall, yhi, ylo,
    sgbuf_y, sgbuf_q, cgbuf, hbuf_z, hbuf_y, hbuf_q, vsend, vrecv, vfull, fbuf, inv1,
    slab_sem, ps, pr, ss, sr, gs, gr, ns, nr, ws, wr, cs, cr, hs, hr, vs, vr, as_, ar, fs, fr,
):
    c = lax.axis_index("cuts")
    l = lax.axis_index("col")
    z, x = l // 2, l % 2
    y, q = c // 4, c % 4

    def col_to(src, dst, s, r, where):
        return pltpu.make_async_remote_copy(
            src_ref=src, dst_ref=dst, send_sem=s, recv_sem=r,
            device_id={"col": where}, device_id_type=MESH,
        )

    def cuts_to(src, dst, s, r, where):
        return pltpu.make_async_remote_copy(
            src_ref=src, dst_ref=dst, send_sem=s, recv_sem=r,
            device_id={"cuts": where}, device_id_type=MESH,
        )

    def col_at(d):
        return lax.rem(l + d, COL)

    def cuts_at(d):
        return lax.rem(c + d, CUTS)

    def z_at(d):
        return lax.rem(z + d, 4) * 2 + x

    def y_at(d):
        return lax.rem(y + d, 4) * 4 + q

    def q_at(d):
        return y * 4 + lax.rem(q + d, 4)

    def slab_copy(k):
        return pltpu.make_async_copy(rec_ref.at[k], slab.at[k], slab_sem.at[k])

    def slice_of(t):
        return lax.rem(z + 2 + t // 3, 4) * 3 + t % 3

    def start_slab(t, carry):
        slab_copy(slice_of(t)).start()
        return carry

    lax.fori_loop(0, SLICES, start_slab, 0)

    barrier = pltpu.get_barrier_semaphore()
    for d in range(1, COL):
        pl.semaphore_signal(barrier, inc=1, device_id={"col": col_at(d)}, device_id_type=MESH)
    for d in range(1, CUTS):
        pl.semaphore_signal(barrier, inc=1, device_id={"cuts": cuts_at(d)}, device_id_type=MESH)

    slot = lax.broadcasted_iota(jnp.int32, (SLICES, SLOTS), 1)
    vmask[...] = jnp.where((slot < len_ref[...]) & (mask_ref[...] == 1), 1.0, 0.0)
    weight = weight_ref[...]
    column = column_ref[...]
    c_high, c_low = halves(column)
    cgbuf[l] = dot(column, column, 1, 1)
    sgbuf_y[y] = dot(weight, weight, 0, 0)

    pl.semaphore_wait(barrier, COL + CUTS - 2)

    for d in range(1, COL):
        to = col_at(d)
        col_to(cgbuf.at[l], cgbuf.at[l], cs.at[to], cr.at[l], to).start()
    for d in range(1, 4):
        to = lax.rem(y + d, 4)
        cuts_to(sgbuf_y.at[y], sgbuf_y.at[y], ws.at[0, to], wr.at[0, y], y_at(d)).start()

    c_both = jnp.concatenate([c_high, c_low], axis=0)

    def project(t, carry):
        k = slice_of(t)
        j = lax.rem(k, 3)
        slab_copy(k).wait()
        for h in range(2):
            owner = (k // 3) * 2 + h
            high, low = halves(slab[k, h * HALF:(h + 1) * HALF, :])
            both = fast(c_both, high, 1, 1)
            part = both[:R] + both[R:] + fast(c_high, low, 1, 1)

            @pl.when(owner == l)
            def keep():
                precv[l, j] = part

            @pl.when(owner != l)
            def send():
                psend[owner, j] = part
                col_to(psend.at[owner, j], precv.at[l, j], ps.at[owner, j], pr.at[l, j], owner).start()
        return carry

    lax.fori_loop(0, SLICES, project, 0)

    for d in range(1, 4):
        frm = lax.rem(y + d, 4)
        cuts_to(sgbuf_y.at[frm], sgbuf_y.at[frm], ws.at[0, frm], wr.at[0, frm], y_at(d)).wait_recv()
    sgbuf_q[q] = sgbuf_y[0] + sgbuf_y[1] + sgbuf_y[2] + sgbuf_y[3]
    for d in range(1, 4):
        to = lax.rem(q + d, 4)
        cuts_to(sgbuf_q.at[q], sgbuf_q.at[q], ws.at[1, to], wr.at[1, q], q_at(d)).start()
    for d in range(1, COL):
        frm = col_at(d)
        col_to(cgbuf.at[frm], cgbuf.at[frm], cs.at[frm], cr.at[frm], frm).wait_recv()
    column_gram = cgbuf[0]
    for i in range(1, COL):
        column_gram = column_gram + cgbuf[i]
    for d in range(1, 4):
        frm = lax.rem(q + d, 4)
        cuts_to(sgbuf_q.at[frm], sgbuf_q.at[frm], ws.at[1, frm], wr.at[1, frm], q_at(d)).wait_recv()
    slice_gram = sgbuf_q[0] + sgbuf_q[1] + sgbuf_q[2] + sgbuf_q[3]
    inv1[...] = inverse(slice_gram * column_gram)

    def reduce(j, carry):
        for d in range(1, COL):
            frm = col_at(d)
            col_to(psend.at[frm, j], precv.at[frm, j], ps.at[frm, j], pr.at[frm, j], frm).wait_recv()
        total = precv[0, j]
        for i in range(1, COL):
            total = total + precv[i, j]
        mask = vmask[pl.ds(z * 3 + j, 1), pl.ds(pl.multiple_of(x * HALF, HALF), HALF)]
        total = total * mask
        pall[l, j] = total
        sgram[x, j] = dot(total, total, 1, 1)
        return carry

    lax.fori_loop(0, 3, reduce, 0)

    other = z * 2 + (1 - x)
    gram_copy = col_to(sgram.at[x], sgram.at[x], ss, sr.at[x], other)
    gram_copy.start()
    for d in range(1, COL):
        to = col_at(d)
        col_to(pall.at[l], pall.at[l], gs.at[to], gr.at[l], to).start()
    col_to(sgram.at[1 - x], sgram.at[1 - x], ss, sr.at[1 - x], other).wait_recv()

    rows, cols = iotas((R, R))
    eye = jnp.where(rows == cols, 1.0, 0.0)
    grams, mixes, scales, sums, wrows = [], [], [], [], []
    for j in range(3):
        wrow = weight_ref[pl.ds(z * 3 + j, 1), :]
        s = sgram[0, j] + sgram[1, j]
        mix = core_ref[...] * wrow
        g = dot(dot(mix, s), mix, 1, 1)
        trace = jnp.sum(jnp.where(rows == cols, g, 0.0), axis=(0, 1), keepdims=True) + 1e-06
        grams.append(g / trace)
        mixes.append(mix)
        scales.append(lax.rsqrt(trace))
        sums.append(s)
        wrows.append(wrow)

    def newton(_, carry):
        gs_, ps_ = carry
        next_g, next_p = [], []
        for g, p in zip(gs_, ps_):
            square = dot(g, g)
            next_p.append(1.5 * p - 0.5 * dot(g, p))
            next_g.append(2.25 * g - 1.5 * square + 0.25 * dot(square, g))
        return next_g, next_p

    grams, polys = lax.fori_loop(0, NS_STEPS - 1, newton, (grams, [eye] * 3))
    h_sum = jnp.zeros((R, R), F32)
    for j in range(3):
        poly = 1.5 * polys[j] - 0.5 * dot(grams[j], polys[j])
        turned = dot(mixes[j], poly, 0, 0) * scales[j]
        nall[z, j * R:(j + 1) * R, :] = turned
        h_sum = h_sum + dot(turned, sums[j], 0, 0) * wrows[j]
    hbuf_z[z] = h_sum
    for d in range(1, 4):
        to = lax.rem(z + d, 4)
        col_to(hbuf_z.at[z], hbuf_z.at[z], hs.at[0, to], hr.at[0, z], z_at(d)).start()
    for d in range(1, 4):
        to = lax.rem(z + d, 4)
        col_to(nall.at[z], nall.at[z], ns.at[to], nr.at[z], z_at(d)).start()

    for d in range(1, COL):
        frm = col_at(d)
        col_to(pall.at[frm], pall.at[frm], gs.at[frm], gr.at[frm], frm).wait_recv()

    def second(k, carry):
        zz, j = k // 3, lax.rem(k, 3)
        acc = jnp.zeros((R, WIDTH), F32)
        for h in range(2):
            high, low = halves(slab[k, h * HALF:(h + 1) * HALF, :])
            acc = acc + three(pall[zz * 2 + h, j], high, low)
        high, low = halves(acc)
        at = pl.ds(pl.multiple_of(k * R, R), R)
        yhi[at, :] = high
        ylo[at, :] = low
        return carry

    lax.fori_loop(0, 4, second, 0)
    for d in range(1, 4):
        frm = lax.rem(z + d, 4)
        col_to(hbuf_z.at[frm], hbuf_z.at[frm], hs.at[0, frm], hr.at[0, frm], z_at(d)).wait_recv()
    hbuf_y[y] = hbuf_z[0] + hbuf_z[1] + hbuf_z[2] + hbuf_z[3]
    for d in range(1, 4):
        to = lax.rem(y + d, 4)
        cuts_to(hbuf_y.at[y], hbuf_y.at[y], hs.at[1, to], hr.at[1, y], y_at(d)).start()
    lax.fori_loop(4, 8, second, 0)
    for d in range(1, 4):
        frm = lax.rem(y + d, 4)
        cuts_to(hbuf_y.at[frm], hbuf_y.at[frm], hs.at[1, frm], hr.at[1, frm], y_at(d)).wait_recv()
    hbuf_q[q] = hbuf_y[0] + hbuf_y[1] + hbuf_y[2] + hbuf_y[3]
    for d in range(1, 4):
        to = lax.rem(q + d, 4)
        cuts_to(hbuf_q.at[q], hbuf_q.at[q], hs.at[2, to], hr.at[2, q], q_at(d)).start()
    lax.fori_loop(8, SLICES, second, 0)
    for d in range(1, 4):
        frm = lax.rem(z + d, 4)
        col_to(nall.at[frm], nall.at[frm], ns.at[frm], nr.at[frm], z_at(d)).wait_recv()
    for d in range(1, 4):
        frm = lax.rem(q + d, 4)
        cuts_to(hbuf_q.at[frm], hbuf_q.at[frm], hs.at[2, frm], hr.at[2, frm], q_at(d)).wait_recv()
    h_terms = hbuf_q[0] + hbuf_q[1] + hbuf_q[2] + hbuf_q[3]

    core_t = dot(inv1[...], h_terms, 1, 1)
    core_t = core_t * lax.rsqrt(jnp.sum(core_t * core_t, axis=1, keepdims=True) + 1e-06)
    core_gram = dot(core_t, core_t, 1, 1)
    stacked = nall[...].reshape(SLICES * R, R)
    mixed = dot(core_t, stacked, 1, 1)
    k_of, s_of = iotas((SLICES, SLICES * R))
    spread = jnp.where(s_of // R == k_of, 1.0, 0.0)
    weighted = mixed * dot(weight, spread, 0, 0)
    v_local = three(weighted, yhi[...], ylo[...])
    for i in range(CUTS):
        part = v_local[(i // 8) * 32:(i // 8) * 32 + 32, (i % 8) * 128:(i % 8) * 128 + 128]
        vsend[i] = part
    vrecv[c] = vsend[c]
    for d in range(1, CUTS):
        to = cuts_at(d)
        cuts_to(vsend.at[to], vrecv.at[c], vs.at[to], vr.at[c], to).start()
    core_out[...] = dot(eye, core_t, 1, 1) * 8.0
    inv2 = inverse(slice_gram * core_gram)
    for d in range(1, CUTS):
        frm = cuts_at(d)
        cuts_to(vsend.at[frm], vrecv.at[frm], vs.at[frm], vr.at[frm], frm).wait_recv()
    total = vrecv[0]
    for i in range(1, CUTS):
        total = total + vrecv[i]
    vfull[c] = total
    for d in range(1, CUTS):
        to = cuts_at(d)
        cuts_to(vfull.at[c], vfull.at[c], as_.at[to], ar.at[c], to).start()
    for d in range(1, CUTS):
        frm = cuts_at(d)
        cuts_to(vfull.at[frm], vfull.at[frm], as_.at[frm], ar.at[frm], frm).wait_recv()
    v_terms = jnp.concatenate(
        [jnp.concatenate([vfull[i * 8 + b] for b in range(8)], axis=1) for i in range(2)], axis=0
    )
    vt = dot(inv2, v_terms)
    fbuf[l, :R, :] = dot(vt, vt, 1, 1)
    found = mixed * three(vt, yhi[...], ylo[...], 1)
    fbuf[l, R:R + SLICES, :] = dot(spread, found, 1, 1)
    for d in range(1, COL):
        to = col_at(d)
        col_to(fbuf.at[l], fbuf.at[l], fs.at[to], fr.at[l], to).start()
    for d in range(1, COL):
        frm = col_at(d)
        col_to(fbuf.at[frm], fbuf.at[frm], fs.at[frm], fr.at[frm], frm).wait_recv()
    total = fbuf[0]
    for i in range(1, COL):
        total = total + fbuf[i]
    v_gram = total[:R]
    w_terms = total[R:R + SLICES]
    d_row, d_col = diagonals(v_gram)
    n_row, n_col = lax.rsqrt(d_row + 1e-06), lax.rsqrt(d_col + 1e-06)
    column_out[...] = vt * (n_col * (8192.0 ** 0.5))
    inv3 = inverse(core_gram * (v_gram * n_col * n_row))
    weight_out[...] = dot(w_terms * n_row, inv3)

    for d in range(1, COL):
        to = col_at(d)
        col_to(cgbuf.at[l], cgbuf.at[l], cs.at[to], cr.at[l], to).wait_send()
        col_to(pall.at[l], pall.at[l], gs.at[to], gr.at[l], to).wait_send()
        col_to(fbuf.at[l], fbuf.at[l], fs.at[to], fr.at[l], to).wait_send()
        for j in range(3):
            col_to(psend.at[to, j], precv.at[l, j], ps.at[to, j], pr.at[l, j], to).wait_send()
    gram_copy.wait_send()
    for d in range(1, 4):
        to = lax.rem(z + d, 4)
        col_to(hbuf_z.at[z], hbuf_z.at[z], hs.at[0, to], hr.at[0, z], z_at(d)).wait_send()
        col_to(nall.at[z], nall.at[z], ns.at[to], nr.at[z], z_at(d)).wait_send()
        to = lax.rem(y + d, 4)
        cuts_to(sgbuf_y.at[y], sgbuf_y.at[y], ws.at[0, to], wr.at[0, y], y_at(d)).wait_send()
        cuts_to(hbuf_y.at[y], hbuf_y.at[y], hs.at[1, to], hr.at[1, y], y_at(d)).wait_send()
        to = lax.rem(q + d, 4)
        cuts_to(sgbuf_q.at[q], sgbuf_q.at[q], ws.at[1, to], wr.at[1, q], q_at(d)).wait_send()
        cuts_to(hbuf_q.at[q], hbuf_q.at[q], hs.at[2, to], hr.at[2, q], q_at(d)).wait_send()
    for d in range(1, CUTS):
        to = cuts_at(d)
        cuts_to(vsend.at[to], vrecv.at[c], vs.at[to], vr.at[c], to).wait_send()
        cuts_to(vfull.at[c], vfull.at[c], as_.at[to], ar.at[c], to).wait_send()


def shards(records, row_lengths, row_mask, core_init, column_init, weight_init):
    vmem = pl.BlockSpec(memory_space=pltpu.VMEM)
    dma = pltpu.SemaphoreType.DMA
    return pl.pallas_call(
        kernel,
        out_shape=(
            jax.ShapeDtypeStruct((R, R), F32),
            jax.ShapeDtypeStruct((R, WIDTH), F32),
            jax.ShapeDtypeStruct((SLICES, R), F32),
        ),
        in_specs=[pl.BlockSpec(memory_space=pl.ANY)] + [vmem] * 5,
        out_specs=(vmem,) * 3,
        scratch_shapes=[
            pltpu.VMEM((SLICES, SLOTS, WIDTH), F32),
            pltpu.VMEM((SLICES, SLOTS), F32),
            pltpu.VMEM((COL, 3, R, HALF), F32),
            pltpu.VMEM((COL, 3, R, HALF), F32),
            pltpu.VMEM((COL, 3, R, HALF), F32),
            pltpu.VMEM((2, 3, R, R), F32),
            pltpu.VMEM((4, 3 * R, R), F32),
            pltpu.VMEM((SLICES * R, WIDTH), BF16),
            pltpu.VMEM((SLICES * R, WIDTH), BF16),
            pltpu.VMEM((4, R, R), F32),
            pltpu.VMEM((4, R, R), F32),
            pltpu.VMEM((COL, R, R), F32),
            pltpu.VMEM((4, R, R), F32),
            pltpu.VMEM((4, R, R), F32),
            pltpu.VMEM((4, R, R), F32),
            pltpu.VMEM((CUTS, 32, 128), F32),
            pltpu.VMEM((CUTS, 32, 128), F32),
            pltpu.VMEM((CUTS, 32, 128), F32),
            pltpu.VMEM((COL, 80, R), F32),
            pltpu.VMEM((R, R), F32),
            dma((SLICES,)),
            dma((COL, 3)), dma((COL, 3)),
            dma, dma((2,)),
            dma((COL,)), dma((COL,)),
            dma((4,)), dma((4,)),
            dma((2, 4)), dma((2, 4)),
            dma((COL,)), dma((COL,)),
            dma((3, 4)), dma((3, 4)),
            dma((CUTS,)), dma((CUTS,)),
            dma((CUTS,)), dma((CUTS,)),
            dma((COL,)), dma((COL,)),
        ],
        compiler_params=pltpu.CompilerParams(
            collective_id=0, has_side_effects=True, vmem_limit_bytes=60 * 1024 * 1024
        ),
    )(records, row_lengths[:, None], row_mask, core_init, column_init, weight_init)


def solution(mesh):
    in_specs = (
        P("cuts", None, "col"),
        P("cuts"),
        P("cuts", None),
        P(),
        P(None, "col"),
        P("cuts", None),
    )
    out_specs = (P(), P(None, "col"), P("cuts", None))
    return jax.shard_map(shards, mesh=mesh, in_specs=in_specs, out_specs=out_specs, check_vma=False)
```

time: 540 us -> 112 us (0.21); the launches traced: 532 us -> 111 us
  blocking collectives: 234 us -> 0 us
  waiting for transfers between devices: 128 us -> 0 us
  matrix products: 109 us -> 0 us
  Pallas kernels: 0 us -> 105 us
  other arithmetic: 41.7 us -> 0 us
  between operations: 14.8 us -> 0.64 us
    psum x5 -> x0, blocking collectives: 234 us -> none  [the longest x1 70.9 us: shards(): lax.psum(jnp.dot(weight_init.T, weight_init, precision=HP), 'cuts')]
    psum x2 -> x0, waiting for transfers between devices: 127 us -> none  [the longest x1 127 us: shards(): v_terms = lax.psum(v_local, 'cuts')]
    dot_general x27 -> x0, matrix products: 105 us -> none  [the longest x1 30.7 us: shards(): partial_value = jnp.einsum('rj,kij->kri', column_init, masked, precision=HP)]
    pallas_call x0 -> x1, Pallas kernels: none -> 105 us  [shards(): pl.pallas_call(kernel, out_shape=(jax.ShapeDtypeStruct((R, R), F32), jax....]
    another operation x15 -> x0, other arithmetic: 37.6 us -> none  [the longest x9 20.3 us: solve_sym(): lower = jnp.linalg.cholesky(gram)]
  transfers between devices with their start and end apart: 2 -> 0, of which waited for: 1 -> 0; matrix products, arithmetic and copies ran while one was open for 4% -> 0% of each run, Pallas kernels for 0% -> 0%
where the time goes in v1:
time: 112 us; the launch traced here: 111 us
  Pallas kernels  105 us (94%)
  local copies, waits for them, and re-layouts  5.68 us (5%)
    pallas_call x1, Pallas kernels, shards(): pl.pallas_call(kernel, out_shape=(jax.ShapeDtypeStruct((R, R), F32), jax....  105 us
    unnamed x3, local copies, waits for them, and re-layouts  4.34 us

profile of v1, /device:TPU:0, one launch (start us, length us, event | category | flops | bytes accessed | tf_op | source)
XLA Modules:
  0.0 110.9 jit_solution(10012749738795149799)
XLA Ops:
  0.6 1.3 %copy.9.len_ref = s32[12,1]{1,0:T(8,128)} copy(s32[12,1]{0,1:T(1,128)} %bitcast.1) | data formatting | bytes 96 | tf_op jit(solution)/shard_map/broadcast_in_dim | solution.py:423
  2.0 104.6 %shard_map.85 = (f32[64,64]{1,0:T(8,128)}, f32[64,1024]{1,0:T(8,128)}, f32[12,64]{1,0:T(8,128)}) custom-call(f32[12,512,1024]{2,1,0:T(8,128)} %rec_ref.1, s32[12,1]{1,0:T(8,128)} %copy.9.len_ref, s32[12,512]{1,0:T(8,128)} %mask_ref.1, f32[64,64]{1,0:T(8,128)} %core_ref.1, f32[64,1024]{1,0:T(8,128)} %column_ref.1, f32[12,64]{1,0:T(8,128)} %weight_ref.1), custom_call_target="tpu_custom_call" | custom-call | tf_op jit(solution)/shard_map/pallas_call | solution.py:378
  106.5 1.4 %copy.13 = f32[64,64]{1,0:T(8,128)} copy(f32[64,64]{1,0:T(8,128)} %get-tuple-element.6) | data formatting | bytes 32768
  107.9 1.7 %copy.14 = f32[64,1024]{1,0:T(8,128)} copy(f32[64,1024]{1,0:T(8,128)} %get-tuple-element.7) | data formatting | bytes 524288
  109.6 1.3 %copy.15 = f32[12,64]{1,0:T(8,128)} copy(f32[12,64]{1,0:T(8,128)} %get-tuple-element.8) | data formatting | bytes 6144

commit v2 on v1

v2 whole, which is shorter than its diff:
```python
import functools

import jax
import jax.numpy as jnp
from jax import lax
from jax.experimental import pallas as pl
from jax.experimental.pallas import tpu as pltpu
from jax.sharding import PartitionSpec as P

R = 64
NS_STEPS = 8
CUTS = 16
COL = 8
SLICES = 12
SLOTS = 512
WIDTH = 1024
HALF = 256

F32 = jnp.float32
BF16 = jnp.bfloat16
HP = lax.Precision.HIGHEST
MESH = pl.DeviceIdType.MESH


def dot(a, b, ca=1, cb=0, precision=HP):
    return lax.dot_general(
        a, b, (((ca,), (cb,)), ((), ())), precision=precision, preferred_element_type=F32
    )


def fast(a, b, ca=1, cb=0):
    return dot(a, b, ca, cb, lax.Precision.DEFAULT)


def halves(x):
    high = x.astype(BF16)
    return high, (x - high.astype(F32)).astype(BF16)


def three(a, b_high, b_low, cb=0):
    a_high, a_low = halves(a)
    rows = a.shape[0]
    both = fast(jnp.concatenate([a_high, a_low], axis=0), b_high, 1, cb)
    return both[:rows] + both[rows:] + fast(a_high, b_low, 1, cb)


def iotas(shape):
    return lax.broadcasted_iota(jnp.int32, shape, 0), lax.broadcasted_iota(jnp.int32, shape, 1)


def diagonals(a):
    rows, cols = iotas(a.shape)
    kept = jnp.where(rows == cols, a, 0.0)
    return jnp.sum(kept, axis=0, keepdims=True), jnp.sum(kept, axis=1, keepdims=True)


def inverse(gram):
    rows, cols = iotas(gram.shape)
    d_row, d_col = diagonals(gram)
    s_row, s_col = lax.rsqrt(d_row), lax.rsqrt(d_col)

    def sweep(p, a):
        at_row, at_col = rows == p, cols == p
        row = jnp.sum(jnp.where(at_row, a, 0.0), axis=0, keepdims=True)
        col = jnp.sum(jnp.where(at_col, a, 0.0), axis=1, keepdims=True)
        pivot = jnp.sum(jnp.where(rows[:, :1] == p, col, 0.0), axis=0, keepdims=True)
        inv = 1.0 / pivot
        scaled = row * inv
        inner = a - col * scaled
        out = jnp.where(at_row, scaled, jnp.where(at_col, -col * inv, inner))
        return jnp.where(at_row & at_col, inv, out)

    return lax.fori_loop(0, R, sweep, gram * s_col * s_row) * s_col * s_row


def kernel(
    len_ref, rec_ref, mask_ref, core_ref, column_ref, weight_ref,
    total_out, vt_out, core_out, gram_out,
    slab, vmask, keep, xsend, xrecv, zsend, zrecv, z0send, z0recv, x0send, x0recv, pall0, pall12,
    sgram, nall, yhi, ylo,
    sgbuf_y, sgbuf_q, cgbuf_z, cgbuf_x, hbuf_y, hbuf_z, hbuf_q, vsend, vrecv, vfull, fbuf, inv1,
    slab_sem, xs, xr, zs, zr, z0s, z0r, x0s, x0r, ss, sr, gxs, gxr, gzs, gzr, g0s, g0r,
    ns, nr, ws, wr, cs, cr, hs, hr, vs, vr, as_, ar, fs, fr,
):
    c = lax.axis_index("cuts")
    l = lax.axis_index("col")
    z, x = l // 2, l % 2
    y, q = c // 4, c % 4
    other = z * 2 + (1 - x)

    sent = []

    def send(copy):
        copy.start()
        sent.append(copy)

    def col_to(src, dst, s, r, where):
        return pltpu.make_async_remote_copy(
            src_ref=src, dst_ref=dst, send_sem=s, recv_sem=r,
            device_id={"col": where}, device_id_type=MESH,
        )

    def cuts_to(src, dst, s, r, where):
        return pltpu.make_async_remote_copy(
            src_ref=src, dst_ref=dst, send_sem=s, recv_sem=r,
            device_id={"cuts": where}, device_id_type=MESH,
        )

    def col_at(d):
        return lax.rem(l + d, COL)

    def cuts_at(d):
        return lax.rem(c + d, CUTS)

    def z_plus(d):
        return lax.rem(z + d, 4)

    def exchange(buf, s, r, here, axis, stage):
        for d in (2, 1, 3):
            there = lax.rem(here + d, 4)
            if axis == "z":
                go, to = col_to, there * 2 + x
            else:
                go, to = cuts_to, (there * 4 + q if axis == "y" else y * 4 + there)
            if stage == "send":
                send(go(buf.at[here], buf.at[here], s.at[there], r.at[here], to))
            else:
                go(buf.at[there], buf.at[there], s.at[there], r.at[there], to).wait_recv()

    def sum4(buf):
        return (buf[0] + buf[1]) + (buf[2] + buf[3])

    def slab_copy(k):
        return pltpu.make_async_copy(rec_ref.at[k], slab.at[k], slab_sem.at[k])

    far = (2, 1, 3, 0)
    for d in far:
        for j in (1, 2):
            slab_copy(z_plus(d) * 3 + j).start()
    for d in far:
        slab_copy(z_plus(d) * 3).start()

    barrier = pltpu.get_barrier_semaphore()
    pl.semaphore_signal(barrier, inc=1, device_id={"col": other}, device_id_type=MESH)
    for d in range(1, 4):
        for axis, to in (
            ("col", z_plus(d) * 2 + x),
            ("cuts", lax.rem(y + d, 4) * 4 + q),
            ("cuts", y * 4 + lax.rem(q + d, 4)),
        ):
            pl.semaphore_signal(barrier, inc=1, device_id={axis: to}, device_id_type=MESH)

    slot = lax.broadcasted_iota(jnp.int32, (1, SLOTS), 1)
    for k in range(SLICES):
        vmask[k:k + 1, :] = jnp.where((slot < len_ref[k]) & (mask_ref[k:k + 1, :] == 1), 1.0, 0.0)
    weight = weight_ref[...]
    column = column_ref[...]
    c_high, c_low = halves(column)
    c_both = jnp.concatenate([c_high, c_low], axis=0)
    cgbuf_z[z] = dot(column, column, 1, 1)
    sgbuf_y[y] = dot(weight, weight, 0, 0)

    def part_of(k, h):
        high, low = halves(slab[k, pl.ds(pl.multiple_of(h * HALF, HALF), HALF), :])
        both = fast(c_both, high, 1, 1)
        return both[:R] + both[R:] + fast(c_high, low, 1, 1)

    def pair(zz):
        def one(j, carry):
            k = zz * 3 + 1 + j
            slab_copy(k).wait()
            xsend[zz, j] = part_of(k, 1 - x)
            keep[zz, j] = part_of(k, x)
            return carry

        lax.fori_loop(0, 2, one, 0)

    def pair_send(zz):
        send(col_to(xsend.at[zz], xrecv.at[zz], xs.at[zz], xr.at[zz], other))

    def pair_sum(zz):
        col_to(xsend.at[zz], xrecv.at[zz], xs.at[zz], xr.at[zz], other).wait_recv()
        zsend[zz] = keep[zz] + xrecv[zz]

    def pair_pass(zz):
        pair_sum(zz)
        send(col_to(zsend.at[zz], zrecv.at[z], zs.at[zz], zr.at[z], zz * 2 + x))

    def single(zz):
        slab_copy(zz * 3).wait()

        def one(h, carry):
            z0send[zz, h] = part_of(zz * 3, h)
            return carry

        lax.fori_loop(0, 2, one, 0)

    def single_send(zz):
        send(col_to(z0send.at[zz], z0recv.at[z], z0s.at[zz], z0r.at[z], zz * 2 + x))

    pair(z_plus(2))
    pl.semaphore_wait(barrier, 10)
    pair_send(z_plus(2))
    exchange(sgbuf_y, ws.at[0], wr.at[0], y, "y", "send")
    exchange(cgbuf_z, cs, cr, z, "z", "send")
    pair(z_plus(1))
    pair_send(z_plus(1))
    pair(z_plus(3))
    pair_send(z_plus(3))
    pair_pass(z_plus(2))
    exchange(sgbuf_y, ws.at[0], wr.at[0], y, "y", "wait")
    sgbuf_q[q] = sum4(sgbuf_y)
    exchange(sgbuf_q, ws.at[1], wr.at[1], q, "q", "send")
    exchange(cgbuf_z, cs, cr, z, "z", "wait")
    cgbuf_x[x] = sum4(cgbuf_z)
    send(col_to(cgbuf_x.at[x], cgbuf_x.at[x], cs.at[4], cr.at[4], other))
    pair(z)
    pair_send(z)
    pair_pass(z_plus(1))
    single(z_plus(2))
    single_send(z_plus(2))
    pair_pass(z_plus(3))
    single(z_plus(1))
    single_send(z_plus(1))
    single(z_plus(3))
    single_send(z_plus(3))
    single(z)
    pair_sum(z)
    for d in far[:3]:
        zz = z_plus(d)
        col_to(z0send.at[zz], z0recv.at[zz], z0s.at[zz], z0r.at[zz], zz * 2 + x).wait_recv()
    x0send[...] = (z0send[z] + z0recv[z_plus(1)]) + (z0recv[z_plus(2)] + z0recv[z_plus(3)])
    send(col_to(x0send, x0recv, x0s, x0r, other))

    def mask_of(j, h):
        return vmask[pl.ds(z * 3 + j, 1), pl.ds(pl.multiple_of(h * HALF, HALF), HALF)]

    for d in far[:3]:
        zz = z_plus(d)
        col_to(zsend.at[zz], zrecv.at[zz], zs.at[zz], zr.at[zz], zz * 2 + x).wait_recv()
    for j in range(2):
        total = (zsend[z, j] + zrecv[z_plus(1), j]) + (zrecv[z_plus(2), j] + zrecv[z_plus(3), j])
        total = total * mask_of(1 + j, x)
        pall12[z, x, j] = total
        sgram[x, j] = dot(total, total, 1, 1)
    send(col_to(sgram.at[x], sgram.at[x], ss, sr.at[x], other))
    send(col_to(pall12.at[z, x], pall12.at[z, x], gxs.at[z], gxr.at[z], other))
    for d in far[:3]:
        zz = z_plus(d)
        send(col_to(pall12.at[z, x], pall12.at[z, x], gzs.at[zz], gzr.at[z], zz * 2 + x))

    exchange(sgbuf_q, ws.at[1], wr.at[1], q, "q", "wait")
    slice_gram = sum4(sgbuf_q)
    col_to(cgbuf_x.at[1 - x], cgbuf_x.at[1 - x], cs.at[4], cr.at[4], other).wait_recv()
    inv1[...] = inverse(slice_gram * (cgbuf_x[0] + cgbuf_x[1]))

    col_to(x0send, x0recv, x0s, x0r, other).wait_recv()
    gram0 = jnp.zeros((R, R), F32)
    for h in range(2):
        total = (x0send[h] + x0recv[h]) * mask_of(0, h)
        pall0[z, h] = total
        gram0 = gram0 + dot(total, total, 1, 1)
    for d in far[:3]:
        zz = z_plus(d)
        send(col_to(pall0.at[z], pall0.at[z], g0s.at[zz], g0r.at[z], zz * 2 + x))
    col_to(sgram.at[1 - x], sgram.at[1 - x], ss, sr.at[1 - x], other).wait_recv()

    rows, cols = iotas((R, R))
    eye = jnp.where(rows == cols, 1.0, 0.0)
    sums = [gram0, sgram[0, 0] + sgram[1, 0], sgram[0, 1] + sgram[1, 1]]
    grams, mixes, scales, wrows = [], [], [], []
    for j in range(3):
        wrow = weight_ref[pl.ds(z * 3 + j, 1), :]
        mix = core_ref[...] * wrow
        g = dot(dot(mix, sums[j]), mix, 1, 1)
        trace = jnp.sum(jnp.where(rows == cols, g, 0.0), axis=(0, 1), keepdims=True) + 1e-06
        grams.append(g / trace)
        mixes.append(mix)
        scales.append(lax.rsqrt(trace))
        wrows.append(wrow)

    def newton(_, carry):
        gs_, ps_ = carry
        next_g, next_p = [], []
        for g, p in zip(gs_, ps_):
            square = dot(g, g)
            next_p.append(1.5 * p - 0.5 * dot(g, p))
            next_g.append(2.25 * g - 1.5 * square + 0.25 * dot(square, g))
        return next_g, next_p

    def forward(d):
        zz = z_plus(d)
        col_to(pall12.at[zz, x], pall12.at[zz, x], gzs.at[zz], gzr.at[zz], zz * 2 + x).wait_recv()
        send(col_to(pall12.at[zz, x], pall12.at[zz, x], gxs.at[zz], gxr.at[zz], other))

    state = lax.fori_loop(0, 3, newton, (grams, [eye] * 3))
    forward(1)
    forward(3)
    state = lax.fori_loop(3, NS_STEPS - 1, newton, state)
    forward(2)
    grams, polys = state
    h_sum = jnp.zeros((R, R), F32)
    for j in range(3):
        poly = 1.5 * polys[j] - 0.5 * dot(grams[j], polys[j])
        turned = dot(mixes[j], poly, 0, 0) * scales[j]
        nall[z, j * R:(j + 1) * R, :] = turned
        h_sum = h_sum + dot(turned, sums[j], 0, 0) * wrows[j]
    hbuf_y[y] = h_sum
    exchange(hbuf_y, hs.at[0], hr.at[0], y, "y", "send")
    exchange(nall, ns, nr, z, "z", "send")

    def second(k, proj):
        acc = jnp.zeros((R, WIDTH), F32)
        for h in range(2):
            high, low = halves(slab[k, h * HALF:(h + 1) * HALF, :])
            acc = acc + three(proj(h), high, low)
        high, low = halves(acc)
        at = pl.ds(pl.multiple_of(k * R, R), R)
        yhi[at, :] = high
        ylo[at, :] = low

    def second0(zz):
        second(zz * 3, lambda h: pall0[zz, h])

    def second12(zz):
        col_to(pall12.at[zz, 1 - x], pall12.at[zz, 1 - x], gxs.at[zz], gxr.at[zz], other).wait_recv()

        def one(j, carry):
            second(zz * 3 + 1 + j, lambda h: pall12[zz, h, j])
            return carry

        lax.fori_loop(0, 2, one, 0)

    second0(z)
    second12(z)
    exchange(hbuf_y, hs.at[0], hr.at[0], y, "y", "wait")
    hbuf_z[z] = sum4(hbuf_y)
    exchange(hbuf_z, hs.at[1], hr.at[1], z, "z", "send")
    exchange(pall0, g0s, g0r, z, "z", "wait")

    def rest0(d, carry):
        second0(z_plus(d))
        return carry

    lax.fori_loop(1, 4, rest0, 0)
    exchange(hbuf_z, hs.at[1], hr.at[1], z, "z", "wait")
    hbuf_q[q] = sum4(hbuf_z)
    exchange(hbuf_q, hs.at[2], hr.at[2], q, "q", "send")
    for d in (1, 3, 2):
        second12(z_plus(d))
    exchange(nall, ns, nr, z, "z", "wait")
    exchange(hbuf_q, hs.at[2], hr.at[2], q, "q", "wait")
    h_terms = sum4(hbuf_q)

    core_t = dot(inv1[...], h_terms, 1, 1)
    core_t = core_t * lax.rsqrt(jnp.sum(core_t * core_t, axis=1, keepdims=True) + 1e-06)
    core_gram = dot(core_t, core_t, 1, 1)
    stacked = nall[...].reshape(SLICES * R, R)
    mixed = dot(core_t, stacked, 1, 1)
    k_of, s_of = iotas((SLICES, SLICES * R))
    spread = jnp.where(s_of // R == k_of, 1.0, 0.0)
    weighted = mixed * dot(weight, spread, 0, 0)
    v_local = three(weighted, yhi[...], ylo[...])
    for i in range(CUTS):
        part = v_local[(i // 8) * 32:(i // 8) * 32 + 32, (i % 8) * 128:(i % 8) * 128 + 128]
        vsend[i] = part
    vrecv[c] = vsend[c]
    for d in range(1, CUTS):
        to = cuts_at(d)
        send(cuts_to(vsend.at[to], vrecv.at[c], vs.at[to], vr.at[c], to))
    core_out[...] = dot(eye, core_t, 1, 1) * 8.0
    gram_out[...] = core_gram
    inv2 = inverse(sum4(sgbuf_q) * core_gram)
    for d in range(1, CUTS):
        frm = cuts_at(d)
        cuts_to(vsend.at[frm], vrecv.at[frm], vs.at[frm], vr.at[frm], frm).wait_recv()
    total = vrecv[0]
    for i in range(1, CUTS):
        total = total + vrecv[i]
    vfull[c] = total
    for d in range(1, CUTS):
        to = cuts_at(d)
        send(cuts_to(vfull.at[c], vfull.at[c], as_.at[to], ar.at[c], to))
    for d in range(1, CUTS):
        frm = cuts_at(d)
        cuts_to(vfull.at[frm], vfull.at[frm], as_.at[frm], ar.at[frm], frm).wait_recv()
    v_terms = jnp.concatenate(
        [jnp.concatenate([vfull[i * 8 + b] for b in range(8)], axis=1) for i in range(2)], axis=0
    )
    vt = dot(inv2, v_terms)
    fbuf[l, :R, :] = dot(vt, vt, 1, 1)
    found = mixed * three(vt, yhi[...], ylo[...], 1)
    fbuf[l, R:, :] = jnp.concatenate([dot(spread, found, 1, 1), jnp.zeros((4, R), F32)], axis=0)
    for d in range(1, COL):
        to = col_at(d)
        send(col_to(fbuf.at[l], fbuf.at[l], fs.at[to], fr.at[l], to))
    vt_out[...] = vt
    for d in range(1, COL):
        frm = col_at(d)
        col_to(fbuf.at[frm], fbuf.at[frm], fs.at[frm], fr.at[frm], frm).wait_recv()
    total = fbuf[0]
    for i in range(1, COL):
        total = total + fbuf[i]
    total_out[...] = total

    for copy in sent:
        copy.wait_send()


def finish(total_ref, vt_ref, core_t_ref, gram_ref, core_out, column_out, weight_out):
    total = total_ref[...]
    v_gram = total[:R]
    w_terms = total[R:R + SLICES]
    d_row, d_col = diagonals(v_gram)
    n_row, n_col = lax.rsqrt(d_row + 1e-06), lax.rsqrt(d_col + 1e-06)
    core_out[...] = core_t_ref[...]
    column_out[...] = vt_ref[...] * (n_col * (8192.0 ** 0.5))
    inv3 = inverse(gram_ref[...] * (v_gram * n_col * n_row))
    weight_out[...] = dot(w_terms * n_row, inv3)


def shards(records, row_lengths, row_mask, core_init, column_init, weight_init):
    vmem = pl.BlockSpec(memory_space=pltpu.VMEM)
    dma = pltpu.SemaphoreType.DMA
    four = dma((4,))
    chunk = pltpu.VMEM((4, 2, R, HALF), F32)
    square = jax.ShapeDtypeStruct((R, R), F32)
    found = pl.pallas_call(
        kernel,
        out_shape=(
            jax.ShapeDtypeStruct((80, R), F32),
            jax.ShapeDtypeStruct((R, WIDTH), F32),
            square,
            square,
        ),
        in_specs=[pl.BlockSpec(memory_space=pltpu.SMEM), pl.BlockSpec(memory_space=pl.ANY)] + [vmem] * 4,
        out_specs=(vmem,) * 4,
        scratch_shapes=[
            pltpu.VMEM((SLICES, SLOTS, WIDTH), F32),
            pltpu.VMEM((SLICES, SLOTS), F32),
            chunk, chunk, chunk,
            chunk, chunk, chunk, chunk,
            pltpu.VMEM((2, R, HALF), F32),
            pltpu.VMEM((2, R, HALF), F32),
            chunk,
            pltpu.VMEM((4, 2, 2, R, HALF), F32),
            pltpu.VMEM((2, 2, R, R), F32),
            pltpu.VMEM((4, 3 * R, R), F32),
            pltpu.VMEM((SLICES * R, WIDTH), BF16),
            pltpu.VMEM((SLICES * R, WIDTH), BF16),
            pltpu.VMEM((4, R, R), F32),
            pltpu.VMEM((4, R, R), F32),
            pltpu.VMEM((4, R, R), F32),
            pltpu.VMEM((2, R, R), F32),
            pltpu.VMEM((4, R, R), F32),
            pltpu.VMEM((4, R, R), F32),
            pltpu.VMEM((4, R, R), F32),
            pltpu.VMEM((CUTS, 32, 128), F32),
            pltpu.VMEM((CUTS, 32, 128), F32),
            pltpu.VMEM((CUTS, 32, 128), F32),
            pltpu.VMEM((COL, 80, R), F32),
            pltpu.VMEM((R, R), F32),
            dma((SLICES,)),
            four, four, four, four, four, four,
            dma, dma,
            dma, dma((2,)),
            four, four, four, four, four, four,
            four, four,
            dma((2, 4)), dma((2, 4)),
            dma((5,)), dma((5,)),
            dma((3, 4)), dma((3, 4)),
            dma((CUTS,)), dma((CUTS,)),
            dma((CUTS,)), dma((CUTS,)),
            dma((COL,)), dma((COL,)),
        ],
        compiler_params=pltpu.CompilerParams(
            collective_id=0, has_side_effects=True, vmem_limit_bytes=60 * 1024 * 1024
        ),
    )(row_lengths, records, row_mask, core_init, column_init, weight_init)
    return pl.pallas_call(
        finish,
        out_shape=(
            square,
            jax.ShapeDtypeStruct((R, WIDTH), F32),
            jax.ShapeDtypeStruct((SLICES, R), F32),
        ),
        in_specs=[vmem] * 4,
        out_specs=(vmem,) * 3,
    )(*found)


def solution(mesh):
    in_specs = (
        P("cuts", None, "col"),
        P("cuts"),
        P("cuts", None),
        P(),
        P(None, "col"),
        P("cuts", None),
    )
    out_specs = (P(), P(None, "col"), P("cuts", None))
    return jax.shard_map(shards, mesh=mesh, in_specs=in_specs, out_specs=out_specs, check_vma=False)
```

time: 112 us -> 88.3 us (0.79)
  Pallas kernels: 105 us -> 86.5 us
  local copies, waits for them, and re-layouts: 5.68 us -> 0 us
    pallas_call x1 -> x2, Pallas kernels: 105 us -> 86.5 us  [the longest x1 77.7 us: shards(): pl.pallas_call(kernel, out_shape=(jax.ShapeDtypeStruct((80, R), F32), jax...]
    unnamed x3 -> x0, local copies, waits for them, and re-layouts: 4.34 us -> none
    broadcast_in_dim x1 -> x0, local copies, waits for them, and re-layouts: 1.34 us -> none  [shards(): row_lengths[:, None]]
where the time goes in v2:
time: 88.3 us; the launch traced here: 87.1 us
  Pallas kernels  86.5 us (98%)
    pallas_call x1, Pallas kernels, shards(): pl.pallas_call(kernel, out_shape=(jax.ShapeDtypeStruct((80, R), F32), jax...  77.7 us
    pallas_call x1, Pallas kernels, shards(): pl.pallas_call(finish, out_shape=(square, jax.ShapeDtypeStruct((R, WIDTH)...  8.79 us

profile of v2, /device:TPU:0, one launch (start us, length us, event | category | flops | bytes accessed | tf_op | source)
XLA Modules:
  0.0 87.1 jit_solution(8615327915098204500)
XLA Ops:
  0.6 77.7 %shard_map.85 = (f32[80,64]{1,0:T(8,128)}, f32[64,1024]{1,0:T(8,128)}, f32[64,64]{1,0:T(8,128)}, f32[64,64]{1,0:T(8,128)}) custom-call(s32[12]{0:T(128)} %len_ref.1, f32[12,512,1024]{2,1,0:T(8,128)} %rec_ref.1, s32[12,512]{1,0:T(8,128)} %mask_ref.1, f32[64,64]{1,0:T(8,128)} %core_ref.1, f32[64,1024]{1,0:T(8,128)} %column_ref.1, f32[12,64]{1,0:T(8,128)} %weight_ref.1), custom_call_target="tpu_custom_call" | custom-call | tf_op jit(solution)/shard_map/pallas_call | solution.py:428
  78.3 8.8 %shard_map.86 = (f32[64,64]{1,0:T(8,128)}, f32[64,1024]{1,0:T(8,128)}, f32[12,64]{1,0:T(8,128)}) custom-call(f32[80,64]{1,0:T(8,128)} %get-tuple-element.7.total_ref, f32[64,1024]{1,0:T(8,128)} %get-tuple-element.8.vt_ref, f32[64,64]{1,0:T(8,128)} %get-tuple-element.9.core_t_ref, f32[64,64]{1,0:T(8,128)} %get-tuple-element.10.gram_ref), custom_call_target="tpu_custom_call" | custom-call | tf_op jit(solution)/shard_map/pallas_call | solution.py:480

commit v3 on v2

--- a/solution.py
+++ b/solution.py
@@ -48,6 +48,15 @@
     return lax.broadcasted_iota(jnp.int32, shape, 0), lax.broadcasted_iota(jnp.int32, shape, 1)
 
 
+def pack(a):
+    half = a.shape[0] // 2
+    return jnp.concatenate([a[:half], a[half:]], axis=1)
+
+
+def unpack(a):
+    return jnp.concatenate([a[:, :R], a[:, R:]], axis=0)
+
+
 def diagonals(a):
     rows, cols = iotas(a.shape)
     kept = jnp.where(rows == cols, a, 0.0)
@@ -59,18 +68,33 @@
     d_row, d_col = diagonals(gram)
     s_row, s_col = lax.rsqrt(d_row), lax.rsqrt(d_col)
 
-    def sweep(p, a):
-        at_row, at_col = rows == p, cols == p
-        row = jnp.sum(jnp.where(at_row, a, 0.0), axis=0, keepdims=True)
-        col = jnp.sum(jnp.where(at_col, a, 0.0), axis=1, keepdims=True)
-        pivot = jnp.sum(jnp.where(rows[:, :1] == p, col, 0.0), axis=0, keepdims=True)
-        inv = 1.0 / pivot
-        scaled = row * inv
-        inner = a - col * scaled
-        out = jnp.where(at_row, scaled, jnp.where(at_col, -col * inv, inner))
-        return jnp.where(at_row & at_col, inv, out)
-
-    return lax.fori_loop(0, R, sweep, gram * s_col * s_row) * s_col * s_row
+    def sweep(t, a):
+        at = [4 * t + i for i in range(4)]
+        r = [jnp.sum(jnp.where(rows == p, a, 0.0), axis=0, keepdims=True) for p in at]
+        c = [jnp.sum(jnp.where(cols == p, a, 0.0), axis=1, keepdims=True) for p in at]
+
+        def pivot(m, n):
+            return jnp.sum(jnp.where(rows[:, :1] == at[m], c[n], 0.0), axis=0, keepdims=True)
+
+        a00, a01, a11 = pivot(0, 0), pivot(0, 1), pivot(1, 1)
+        b00, b01, b10, b11 = pivot(0, 2), pivot(0, 3), pivot(1, 2), pivot(1, 3)
+        k = 1.0 / (a00 * a11 - a01 * a01)
+        i00, i01, i11 = a11 * k, -a01 * k, a00 * k
+        t00, t01 = i00 * b00 + i01 * b10, i00 * b01 + i01 * b11
+        t10, t11 = i01 * b00 + i11 * b10, i01 * b01 + i11 * b11
+        s0 = pivot(2, 2) - (b00 * t00 + b10 * t10)
+        s1 = pivot(2, 3) - (b00 * t01 + b10 * t11)
+        s2 = pivot(3, 3) - (b01 * t01 + b11 * t11)
+        m = 1.0 / (s0 * s2 - s1 * s1)
+        r = [v + jnp.where(cols[:1] == p, 1.0, 0.0) for v, p in zip(r, at)]
+        c = [v - jnp.where(rows[:, :1] == p, 1.0, 0.0) for v, p in zip(c, at)]
+        y0, y1 = i00 * r[0] + i01 * r[1], i01 * r[0] + i11 * r[1]
+        z0, z1 = r[2] - (b00 * y0 + b10 * y1), r[3] - (b01 * y0 + b11 * y1)
+        u2, u3 = (s2 * m) * z0 - (s1 * m) * z1, (s0 * m) * z1 - (s1 * m) * z0
+        u0, u1 = y0 - (t00 * u2 + t01 * u3), y1 - (t10 * u2 + t11 * u3)
+        return a - ((c[0] * u0 + c[1] * u1) + (c[2] * u2 + c[3] * u3))
+
+    return lax.fori_loop(0, R // 4, sweep, gram * s_col * s_row) * s_col * s_row
 
 
 def kernel(
@@ -78,7 +102,7 @@
     total_out, vt_out, core_out, gram_out,
     slab, vmask, keep, xsend, xrecv, zsend, zrecv, z0send, z0recv, x0send, x0recv, pall0, pall12,
     sgram, nall, yhi, ylo,
-    sgbuf_y, sgbuf_q, cgbuf_z, cgbuf_x, hbuf_y, hbuf_z, hbuf_q, vsend, vrecv, vfull, fbuf, inv1,
+    sgbuf_y, sgbuf_q, cgbuf_z, cgbuf_x, hbuf_y, hbuf_z, hbuf_q, vsend, vrecv, vfull, fbuf, inv1, slice_gram, wide,
     slab_sem, xs, xr, zs, zr, z0s, z0r, x0s, x0r, ss, sr, gxs, gxr, gzs, gzr, g0s, g0r,
     ns, nr, ws, wr, cs, cr, hs, hr, vs, vr, as_, ar, fs, fr,
 ):
@@ -134,11 +158,8 @@
         return pltpu.make_async_copy(rec_ref.at[k], slab.at[k], slab_sem.at[k])
 
     far = (2, 1, 3, 0)
-    for d in far:
-        for j in (1, 2):
-            slab_copy(z_plus(d) * 3 + j).start()
-    for d in far:
-        slab_copy(z_plus(d) * 3).start()
+    for d, j in ((2, 0), (2, 1), (2, 2), (1, 1), (1, 2), (1, 0), (3, 1), (3, 2), (3, 0), (0, 1), (0, 2), (0, 0)):
+        slab_copy(z_plus(d) * 3 + j).start()
 
     barrier = pltpu.get_barrier_semaphore()
     pl.semaphore_signal(barrier, inc=1, device_id={"col": other}, device_id_type=MESH)
@@ -157,8 +178,8 @@
     column = column_ref[...]
     c_high, c_low = halves(column)
     c_both = jnp.concatenate([c_high, c_low], axis=0)
-    cgbuf_z[z] = dot(column, column, 1, 1)
-    sgbuf_y[y] = dot(weight, weight, 0, 0)
+    cgbuf_z[z] = pack(dot(column, column, 1, 1))
+    sgbuf_y[y] = pack(dot(weight, weight, 0, 0))
 
     def part_of(k, h):
         high, low = halves(slab[k, pl.ds(pl.multiple_of(h * HALF, HALF), HALF), :])
@@ -198,39 +219,39 @@
     def single_send(zz):
         send(col_to(z0send.at[zz], z0recv.at[z], z0s.at[zz], z0r.at[z], zz * 2 + x))
 
+    single(z_plus(2))
+    pl.semaphore_wait(barrier, 10)
+    single_send(z_plus(2))
     pair(z_plus(2))
-    pl.semaphore_wait(barrier, 10)
     pair_send(z_plus(2))
     exchange(sgbuf_y, ws.at[0], wr.at[0], y, "y", "send")
     exchange(cgbuf_z, cs, cr, z, "z", "send")
     pair(z_plus(1))
     pair_send(z_plus(1))
+    single(z_plus(1))
+    single_send(z_plus(1))
+    pair_pass(z_plus(2))
     pair(z_plus(3))
     pair_send(z_plus(3))
-    pair_pass(z_plus(2))
     exchange(sgbuf_y, ws.at[0], wr.at[0], y, "y", "wait")
     sgbuf_q[q] = sum4(sgbuf_y)
     exchange(sgbuf_q, ws.at[1], wr.at[1], q, "q", "send")
+    single(z_plus(3))
+    single_send(z_plus(3))
+    pair_pass(z_plus(1))
     exchange(cgbuf_z, cs, cr, z, "z", "wait")
     cgbuf_x[x] = sum4(cgbuf_z)
     send(col_to(cgbuf_x.at[x], cgbuf_x.at[x], cs.at[4], cr.at[4], other))
     pair(z)
     pair_send(z)
-    pair_pass(z_plus(1))
-    single(z_plus(2))
-    single_send(z_plus(2))
+    single(z)
     pair_pass(z_plus(3))
-    single(z_plus(1))
-    single_send(z_plus(1))
-    single(z_plus(3))
-    single_send(z_plus(3))
-    single(z)
-    pair_sum(z)
     for d in far[:3]:
         zz = z_plus(d)
         col_to(z0send.at[zz], z0recv.at[zz], z0s.at[zz], z0r.at[zz], zz * 2 + x).wait_recv()
     x0send[...] = (z0send[z] + z0recv[z_plus(1)]) + (z0recv[z_plus(2)] + z0recv[z_plus(3)])
     send(col_to(x0send, x0recv, x0s, x0r, other))
+    pair_sum(z)
 
     def mask_of(j, h):
         return vmask[pl.ds(z * 3 + j, 1), pl.ds(pl.multiple_of(h * HALF, HALF), HALF)]
@@ -238,22 +259,26 @@
     for d in far[:3]:
         zz = z_plus(d)
         col_to(zsend.at[zz], zrecv.at[zz], zs.at[zz], zr.at[zz], zz * 2 + x).wait_recv()
+    partial_grams = []
     for j in range(2):
         total = (zsend[z, j] + zrecv[z_plus(1), j]) + (zrecv[z_plus(2), j] + zrecv[z_plus(3), j])
         total = total * mask_of(1 + j, x)
         pall12[z, x, j] = total
-        sgram[x, j] = dot(total, total, 1, 1)
+        partial_grams.append(dot(total, total, 1, 1))
+    sgram[x] = jnp.concatenate(partial_grams, axis=1)
     send(col_to(sgram.at[x], sgram.at[x], ss, sr.at[x], other))
-    send(col_to(pall12.at[z, x], pall12.at[z, x], gxs.at[z], gxr.at[z], other))
-    for d in far[:3]:
+    for d in (1, 3, 2):
         zz = z_plus(d)
         send(col_to(pall12.at[z, x], pall12.at[z, x], gzs.at[zz], gzr.at[z], zz * 2 + x))
+    send(col_to(pall12.at[z, x], pall12.at[z, x], gxs.at[z], gxr.at[z], other))
 
     exchange(sgbuf_q, ws.at[1], wr.at[1], q, "q", "wait")
-    slice_gram = sum4(sgbuf_q)
+    slice_gram[...] = unpack(sum4(sgbuf_q))
     col_to(cgbuf_x.at[1 - x], cgbuf_x.at[1 - x], cs.at[4], cr.at[4], other).wait_recv()
-    inv1[...] = inverse(slice_gram * (cgbuf_x[0] + cgbuf_x[1]))
-
+    inv1[...] = inverse(slice_gram[...] * unpack(cgbuf_x[0] + cgbuf_x[1]))
+    k_of, s_of = iotas((SLICES, SLICES * R))
+    spread = jnp.where(s_of // R == k_of, 1.0, 0.0)
+    wide[...] = dot(weight, spread, 0, 0)
     col_to(x0send, x0recv, x0s, x0r, other).wait_recv()
     gram0 = jnp.zeros((R, R), F32)
     for h in range(2):
@@ -267,7 +292,8 @@
 
     rows, cols = iotas((R, R))
     eye = jnp.where(rows == cols, 1.0, 0.0)
-    sums = [gram0, sgram[0, 0] + sgram[1, 0], sgram[0, 1] + sgram[1, 1]]
+    both = sgram[0] + sgram[1]
+    sums = [gram0, both[:, :R], both[:, R:]]
     grams, mixes, scales, wrows = [], [], [], []
     for j in range(3):
         wrow = weight_ref[pl.ds(z * 3 + j, 1), :]
@@ -300,12 +326,14 @@
     forward(2)
     grams, polys = state
     h_sum = jnp.zeros((R, R), F32)
+    turned_all = []
     for j in range(3):
         poly = 1.5 * polys[j] - 0.5 * dot(grams[j], polys[j])
         turned = dot(mixes[j], poly, 0, 0) * scales[j]
-        nall[z, j * R:(j + 1) * R, :] = turned
+        turned_all.append(turned)
         h_sum = h_sum + dot(turned, sums[j], 0, 0) * wrows[j]
-    hbuf_y[y] = h_sum
+    hbuf_y[y] = pack(h_sum)
+    nall[z] = pack(jnp.concatenate(turned_all, axis=0))
     exchange(hbuf_y, hs.at[0], hr.at[0], y, "y", "send")
     exchange(nall, ns, nr, z, "z", "send")
 
@@ -331,35 +359,33 @@
 
         lax.fori_loop(0, 2, one, 0)
 
-    second0(z)
+    exchange(pall0, g0s, g0r, z, "z", "wait")
+
+    def all0(zz, carry):
+        second0(zz)
+        return carry
+
+    lax.fori_loop(0, 4, all0, 0)
     second12(z)
     exchange(hbuf_y, hs.at[0], hr.at[0], y, "y", "wait")
     hbuf_z[z] = sum4(hbuf_y)
     exchange(hbuf_z, hs.at[1], hr.at[1], z, "z", "send")
-    exchange(pall0, g0s, g0r, z, "z", "wait")
-
-    def rest0(d, carry):
-        second0(z_plus(d))
-        return carry
-
-    lax.fori_loop(1, 4, rest0, 0)
+    second12(z_plus(1))
     exchange(hbuf_z, hs.at[1], hr.at[1], z, "z", "wait")
     hbuf_q[q] = sum4(hbuf_z)
     exchange(hbuf_q, hs.at[2], hr.at[2], q, "q", "send")
-    for d in (1, 3, 2):
-        second12(z_plus(d))
+    second12(z_plus(3))
+    second12(z_plus(2))
     exchange(nall, ns, nr, z, "z", "wait")
     exchange(hbuf_q, hs.at[2], hr.at[2], q, "q", "wait")
-    h_terms = sum4(hbuf_q)
+    h_terms = unpack(sum4(hbuf_q))
 
     core_t = dot(inv1[...], h_terms, 1, 1)
     core_t = core_t * lax.rsqrt(jnp.sum(core_t * core_t, axis=1, keepdims=True) + 1e-06)
     core_gram = dot(core_t, core_t, 1, 1)
-    stacked = nall[...].reshape(SLICES * R, R)
+    stacked = jnp.concatenate([unpack(nall[i]) for i in range(4)], axis=0)
     mixed = dot(core_t, stacked, 1, 1)
-    k_of, s_of = iotas((SLICES, SLICES * R))
-    spread = jnp.where(s_of // R == k_of, 1.0, 0.0)
-    weighted = mixed * dot(weight, spread, 0, 0)
+    weighted = mixed * wide[...]
     v_local = three(weighted, yhi[...], ylo[...])
     for i in range(CUTS):
         part = v_local[(i // 8) * 32:(i // 8) * 32 + 32, (i % 8) * 128:(i % 8) * 128 + 128]
@@ -370,7 +396,7 @@
         send(cuts_to(vsend.at[to], vrecv.at[c], vs.at[to], vr.at[c], to))
     core_out[...] = dot(eye, core_t, 1, 1) * 8.0
     gram_out[...] = core_gram
-    inv2 = inverse(sum4(sgbuf_q) * core_gram)
+    inv2 = inverse(slice_gram[...] * core_gram)
     for d in range(1, CUTS):
         frm = cuts_at(d)
         cuts_to(vsend.at[frm], vrecv.at[frm], vs.at[frm], vr.at[frm], frm).wait_recv()
@@ -388,9 +414,10 @@
         [jnp.concatenate([vfull[i * 8 + b] for b in range(8)], axis=1) for i in range(2)], axis=0
     )
     vt = dot(inv2, v_terms)
-    fbuf[l, :R, :] = dot(vt, vt, 1, 1)
+    v_gram = dot(vt, vt, 1, 1)
     found = mixed * three(vt, yhi[...], ylo[...], 1)
-    fbuf[l, R:, :] = jnp.concatenate([dot(spread, found, 1, 1), jnp.zeros((4, R), F32)], axis=0)
+    w_terms = jnp.concatenate([dot(spread, found, 1, 1), jnp.zeros((4, R), F32)], axis=0)
+    fbuf[l] = jnp.concatenate([pack(v_gram), pack(w_terms)], axis=0)
     for d in range(1, COL):
         to = col_at(d)
         send(col_to(fbuf.at[l], fbuf.at[l], fs.at[to], fr.at[l], to))
@@ -409,8 +436,8 @@
 
 def finish(total_ref, vt_ref, core_t_ref, gram_ref, core_out, column_out, weight_out):
     total = total_ref[...]
-    v_gram = total[:R]
-    w_terms = total[R:R + SLICES]
+    v_gram = unpack(total[:32])
+    w_terms = unpack(total[32:])[:SLICES]
     d_row, d_col = diagonals(v_gram)
     n_row, n_col = lax.rsqrt(d_row + 1e-06), lax.rsqrt(d_col + 1e-06)
     core_out[...] = core_t_ref[...]
@@ -428,7 +455,7 @@
     found = pl.pallas_call(
         kernel,
         out_shape=(
-            jax.ShapeDtypeStruct((80, R), F32),
+            jax.ShapeDtypeStruct((40, 128), F32),
             jax.ShapeDtypeStruct((R, WIDTH), F32),
             square,
             square,
@@ -444,22 +471,24 @@
             pltpu.VMEM((2, R, HALF), F32),
             chunk,
             pltpu.VMEM((4, 2, 2, R, HALF), F32),
-            pltpu.VMEM((2, 2, R, R), F32),
-            pltpu.VMEM((4, 3 * R, R), F32),
+            pltpu.VMEM((2, R, 128), F32),
+            pltpu.VMEM((4, 3 * R // 2, 128), F32),
             pltpu.VMEM((SLICES * R, WIDTH), BF16),
             pltpu.VMEM((SLICES * R, WIDTH), BF16),
-            pltpu.VMEM((4, R, R), F32),
-            pltpu.VMEM((4, R, R), F32),
-            pltpu.VMEM((4, R, R), F32),
-            pltpu.VMEM((2, R, R), F32),
-            pltpu.VMEM((4, R, R), F32),
-            pltpu.VMEM((4, R, R), F32),
-            pltpu.VMEM((4, R, R), F32),
+            pltpu.VMEM((4, 32, 128), F32),
+            pltpu.VMEM((4, 32, 128), F32),
+            pltpu.VMEM((4, 32, 128), F32),
+            pltpu.VMEM((2, 32, 128), F32),
+            pltpu.VMEM((4, 32, 128), F32),
+            pltpu.VMEM((4, 32, 128), F32),
+            pltpu.VMEM((4, 32, 128), F32),
             pltpu.VMEM((CUTS, 32, 128), F32),
             pltpu.VMEM((CUTS, 32, 128), F32),
             pltpu.VMEM((CUTS, 32, 128), F32),
-            pltpu.VMEM((COL, 80, R), F32),
+            pltpu.VMEM((COL, 40, 128), F32),
             pltpu.VMEM((R, R), F32),
+            pltpu.VMEM((R, R), F32),
+            pltpu.VMEM((R, SLICES * R), F32),
             dma((SLICES,)),
             four, four, four, four, four, four,
             dma, dma,

time: 88.3 us -> 77.9 us (0.88)
  Pallas kernels: 86.5 us -> 76.7 us
    pallas_call x1, Pallas kernels: 77.7 us -> 72.3 us  [shards(): pl.pallas_call(kernel, out_shape=(jax.ShapeDtypeStruct((40, 128), F32), j...]
    pallas_call x1, Pallas kernels: 8.79 us -> 4.39 us  [shards(): pl.pallas_call(finish, out_shape=(square, jax.ShapeDtypeStruct((R, WIDTH)...]
where the time goes in v3:
time: 77.9 us; the launch traced here: 77.3 us
  Pallas kernels  76.7 us (98%)
    pallas_call x1, Pallas kernels, shards(): pl.pallas_call(kernel, out_shape=(jax.ShapeDtypeStruct((40, 128), F32), j...  72.3 us
    pallas_call x1, Pallas kernels, shards(): pl.pallas_call(finish, out_shape=(square, jax.ShapeDtypeStruct((R, WIDTH)...  4.39 us

profile of v3, /device:TPU:0, one launch (start us, length us, event | category | flops | bytes accessed | tf_op | source)
XLA Modules:
  0.0 77.3 jit_solution(18141673794362216697)
XLA Ops:
  0.6 72.3 %shard_map.85 = (f32[40,128]{1,0:T(8,128)}, f32[64,1024]{1,0:T(8,128)}, f32[64,64]{1,0:T(8,128)}, f32[64,64]{1,0:T(8,128)}) custom-call(s32[12]{0:T(128)} %len_ref.1, f32[12,512,1024]{2,1,0:T(8,128)} %rec_ref.1, s32[12,512]{1,0:T(8,128)} %mask_ref.1, f32[64,64]{1,0:T(8,128)} %core_ref.1, f32[64,1024]{1,0:T(8,128)} %column_ref.1, f32[12,64]{1,0:T(8,128)} %weight_ref.1), custom_call_target="tpu_custom_call" | custom-call | tf_op jit(solution)/shard_map/pallas_call | solution.py:455
  72.9 4.4 %shard_map.86 = (f32[64,64]{1,0:T(8,128)}, f32[64,1024]{1,0:T(8,128)}, f32[12,64]{1,0:T(8,128)}) custom-call(f32[40,128]{1,0:T(8,128)} %get-tuple-element.7.total_ref, f32[64,1024]{1,0:T(8,128)} %get-tuple-element.8.vt_ref, f32[64,64]{1,0:T(8,128)} %get-tuple-element.9.core_t_ref, f32[64,64]{1,0:T(8,128)} %get-tuple-element.10.gram_ref), custom_call_target="tpu_custom_call" | custom-call | tf_op jit(solution)/shard_map/pallas_call | solution.py:509

commit v4 on v3

--- a/solution.py
+++ b/solution.py
@@ -305,30 +305,33 @@
         scales.append(lax.rsqrt(trace))
         wrows.append(wrow)
 
-    def newton(_, carry):
-        gs_, ps_ = carry
-        next_g, next_p = [], []
-        for g, p in zip(gs_, ps_):
-            square = dot(g, g)
-            next_p.append(1.5 * p - 0.5 * dot(g, p))
-            next_g.append(2.25 * g - 1.5 * square + 0.25 * dot(square, g))
-        return next_g, next_p
+    left = lax.broadcasted_iota(jnp.int32, (1, 2 * R), 1) < R
+    by0 = jnp.where(left, 2.25, 1.5)
+    by1 = jnp.where(left, 1.5, 0.5)
+    by2 = jnp.where(left, 0.25, 0.0)
+
+    def newton(_, states):
+        following = []
+        for u in states:
+            once = dot(u[:, :R], u)
+            twice = dot(once[:, :R], u)
+            following.append(by0 * u - by1 * once + by2 * twice)
+        return following
 
     def forward(d):
         zz = z_plus(d)
         col_to(pall12.at[zz, x], pall12.at[zz, x], gzs.at[zz], gzr.at[zz], zz * 2 + x).wait_recv()
         send(col_to(pall12.at[zz, x], pall12.at[zz, x], gxs.at[zz], gxr.at[zz], other))
 
-    state = lax.fori_loop(0, 3, newton, (grams, [eye] * 3))
+    state = lax.fori_loop(0, 3, newton, [jnp.concatenate([g, eye], axis=1) for g in grams])
     forward(1)
     forward(3)
     state = lax.fori_loop(3, NS_STEPS - 1, newton, state)
     forward(2)
-    grams, polys = state
     h_sum = jnp.zeros((R, R), F32)
     turned_all = []
     for j in range(3):
-        poly = 1.5 * polys[j] - 0.5 * dot(grams[j], polys[j])
+        poly = (1.5 * state[j] - 0.5 * dot(state[j][:, :R], state[j]))[:, R:]
         turned = dot(mixes[j], poly, 0, 0) * scales[j]
         turned_all.append(turned)
         h_sum = h_sum + dot(turned, sums[j], 0, 0) * wrows[j]

time: 77.9 us -> 79 us (1.014)
  Pallas kernels: 76.7 us -> 77.8 us
    pallas_call x1, Pallas kernels: 72.3 us -> 73.4 us  [shards(): pl.pallas_call(kernel, out_shape=(jax.ShapeDtypeStruct((40, 128), F32), j...]
where the time goes in v4:
time: 79 us; the launch traced here: 78.4 us
  Pallas kernels  77.8 us (98%)
    pallas_call x1, Pallas kernels, shards(): pl.pallas_call(kernel, out_shape=(jax.ShapeDtypeStruct((40, 128), F32), j...  73.4 us
    pallas_call x1, Pallas kernels, shards(): pl.pallas_call(finish, out_shape=(square, jax.ShapeDtypeStruct((R, WIDTH)...  4.39 us

profile of v4, /device:TPU:0, one launch (start us, length us, event | category | flops | bytes accessed | tf_op | source)
XLA Modules:
  0.0 78.4 jit_solution(14612561265340298)
XLA Ops:
  0.6 73.4 %shard_map.85 = (f32[40,128]{1,0:T(8,128)}, f32[64,1024]{1,0:T(8,128)}, f32[64,64]{1,0:T(8,128)}, f32[64,64]{1,0:T(8,128)}) custom-call(s32[12]{0:T(128)} %len_ref.1, f32[12,512,1024]{2,1,0:T(8,128)} %rec_ref.1, s32[12,512]{1,0:T(8,128)} %mask_ref.1, f32[64,64]{1,0:T(8,128)} %core_ref.1, f32[64,1024]{1,0:T(8,128)} %column_ref.1, f32[12,64]{1,0:T(8,128)} %weight_ref.1), custom_call_target="tpu_custom_call" | custom-call | tf_op jit(solution)/shard_map/pallas_call | solution.py:458
  74.0 4.4 %shard_map.86 = (f32[64,64]{1,0:T(8,128)}, f32[64,1024]{1,0:T(8,128)}, f32[12,64]{1,0:T(8,128)}) custom-call(f32[40,128]{1,0:T(8,128)} %get-tuple-element.7.total_ref, f32[64,1024]{1,0:T(8,128)} %get-tuple-element.8.vt_ref, f32[64,64]{1,0:T(8,128)} %get-tuple-element.9.core_t_ref, f32[64,64]{1,0:T(8,128)} %get-tuple-element.10.gram_ref), custom_call_target="tpu_custom_call" | custom-call | tf_op jit(solution)/shard_map/pallas_call | solution.py:512

commit v5 on v4

--- a/solution.py
+++ b/solution.py
@@ -323,10 +323,10 @@
         col_to(pall12.at[zz, x], pall12.at[zz, x], gzs.at[zz], gzr.at[zz], zz * 2 + x).wait_recv()
         send(col_to(pall12.at[zz, x], pall12.at[zz, x], gxs.at[zz], gxr.at[zz], other))
 
-    state = lax.fori_loop(0, 3, newton, [jnp.concatenate([g, eye], axis=1) for g in grams])
+    state = [jnp.concatenate([g, eye], axis=1) for g in grams]
+    state = lax.fori_loop(0, NS_STEPS - 1, newton, state)
     forward(1)
     forward(3)
-    state = lax.fori_loop(3, NS_STEPS - 1, newton, state)
     forward(2)
     h_sum = jnp.zeros((R, R), F32)
     turned_all = []

time: 79 us -> 77.5 us (0.981)
  Pallas kernels: 77.8 us -> 76.3 us
    pallas_call x1, Pallas kernels: 73.4 us -> 71.9 us  [shards(): pl.pallas_call(kernel, out_shape=(jax.ShapeDtypeStruct((40, 128), F32), j...]
where the time goes in v5:
time: 77.5 us; the launch traced here: 76.9 us
  Pallas kernels  76.3 us (98%)
    pallas_call x1, Pallas kernels, shards(): pl.pallas_call(kernel, out_shape=(jax.ShapeDtypeStruct((40, 128), F32), j...  71.9 us
    pallas_call x1, Pallas kernels, shards(): pl.pallas_call(finish, out_shape=(square, jax.ShapeDtypeStruct((R, WIDTH)...  4.39 us

profile of v5, /device:TPU:0, one launch (start us, length us, event | category | flops | bytes accessed | tf_op | source)
XLA Modules:
  0.0 76.9 jit_solution(2161684434031018543)
XLA Ops:
  0.6 71.9 %shard_map.85 = (f32[40,128]{1,0:T(8,128)}, f32[64,1024]{1,0:T(8,128)}, f32[64,64]{1,0:T(8,128)}, f32[64,64]{1,0:T(8,128)}) custom-call(s32[12]{0:T(128)} %len_ref.1, f32[12,512,1024]{2,1,0:T(8,128)} %rec_ref.1, s32[12,512]{1,0:T(8,128)} %mask_ref.1, f32[64,64]{1,0:T(8,128)} %core_ref.1, f32[64,1024]{1,0:T(8,128)} %column_ref.1, f32[12,64]{1,0:T(8,128)} %weight_ref.1), custom_call_target="tpu_custom_call" | custom-call | tf_op jit(solution)/shard_map/pallas_call | solution.py:458
  72.5 4.4 %shard_map.86 = (f32[64,64]{1,0:T(8,128)}, f32[64,1024]{1,0:T(8,128)}, f32[12,64]{1,0:T(8,128)}) custom-call(f32[40,128]{1,0:T(8,128)} %get-tuple-element.7.total_ref, f32[64,1024]{1,0:T(8,128)} %get-tuple-element.8.vt_ref, f32[64,64]{1,0:T(8,128)} %get-tuple-element.9.core_t_ref, f32[64,64]{1,0:T(8,128)} %get-tuple-element.10.gram_ref), custom_call_target="tpu_custom_call" | custom-call | tf_op jit(solution)/shard_map/pallas_call | solution.py:512
